TPU v7x, 32 devices: a whole 2x2x4 slice. The times are simulated.
32 devices in a mesh: dp: 8 (over z, y), mp: 4 (over x, core).
Axes of the slice: x: 2, y: 2, z: 4, core: 2. Of those that a mesh axis runs over, the one named last changes fastest.
Arguments:
- queries: bfloat16 [1536, 4096], P('dp', 'mp'), as said below
- passages: bfloat16 [512, 4096], P('dp', 'mp'), as said below
- pair_block: int32 [8, 8], P(None, 'dp'), may hold values from 0 to 3
- positives: int32 [1536], P('dp'), may hold values from 0 to 127
Outputs:
- loss: float32 [], replicated
- query_grad: float32 [1536, 4096], P('dp', 'mp')
- passage_grad: float32 [512, 4096], P('dp', 'mp')
Inputs may be any that keep to these rules, and one draw needn't show every extreme that they name: `queries`: query embeddings. `passages`: passage embeddings.
All inputs are finite; a program needn't handle non-finite values.
Results may differ from a plain program's by a relative error of at most 0.0019.
Values may be sent and summed in bfloat16 or wider, within the bound.
A program may use at most 64 MiB of HBM per device.

v0:
```python
import jax
import jax.numpy as jnp
from jax import lax
from jax.sharding import PartitionSpec as P

PBLK = 16
PB_DEV = 4


def weigh(scores, picks):
    top = jnp.max(scores, axis=1, keepdims=True)
    shifted = jnp.exp(scores - top)
    total = jnp.sum(shifted, axis=1, keepdims=True)
    probs = shifted / total
    hits = picks[:, None] == lax.broadcasted_iota(jnp.int32, scores.shape, 1)
    chosen = jnp.sum(jnp.where(hits, scores, 0.0), axis=1)
    losses = top[:, 0] + jnp.log(total[:, 0]) - chosen
    weights = (probs - hits.astype(jnp.float32)).astype(jnp.bfloat16)
    return (weights, jnp.sum(losses))


def per_device(queries, passages, pair_block, positives):
    width = queries.shape[1]
    groups = lax.axis_size("dp")
    owned = passages.reshape(PB_DEV, PBLK, width)
    picked = pair_block[:, 0]
    outgoing = owned[picked]
    incoming = lax.all_to_all(outgoing, "dp", split_axis=0, concat_axis=0, tiled=True)
    flat = incoming.reshape(groups * PBLK, width)
    partial_value = lax.dot_general(
        queries, flat, (((1,), (1,)), ((), ())), preferred_element_type=jnp.float32
    )
    scores = lax.psum(partial_value, "mp")
    weights, loss_sum = weigh(scores, positives)
    loss = lax.psum(loss_sum, "dp") / (queries.shape[0] * groups)
    query_grad = jnp.dot(weights, flat, preferred_element_type=jnp.float32)
    cand_grad = lax.dot_general(
        weights, queries, (((0,), (0,)), ((), ())), preferred_element_type=jnp.float32
    )
    returned = lax.all_to_all(
        cand_grad.reshape(groups, PBLK, width), "dp", split_axis=0, concat_axis=0, tiled=True
    )
    onehot = (picked[:, None] == jnp.arange(PB_DEV, dtype=jnp.int32)[None, :]).astype(jnp.float32)
    summed = jnp.einsum("jk,jrd->krd", onehot, returned, precision=lax.Precision.HIGHEST)
    passage_grad = summed.reshape(PB_DEV * PBLK, width)
    return (loss, query_grad, passage_grad)


def solution(mesh):
    in_specs = (P("dp", "mp"), P("dp", "mp"), P(None, "dp"), P("dp"))
    out_specs = (P(), P("dp", "mp"), P("dp", "mp"))
    return jax.shard_map(
        per_device, mesh=mesh, in_specs=in_specs, out_specs=out_specs, check_vma=False
    )
```

profile of v0, /device:TPU:0, one launch (start us, length us, event | category | flops | bytes accessed | tf_op | source)
XLA Modules:
  0.0 99.9 jit_solution(3494430728572000360)
XLA Ops:
  7.2 0.0 copy-start
  7.2 0.0 all-reduce.2.cloned.1.call-start
  7.2 0.7 fusion.6
  7.9 1.5 %gather_fusion = bf16[8,16,1024]{2,1,0:T(8,128)(2,1)S(1)} fusion(bf16[4,16,1024]{2,1,0:T(8,128)(2,1)} %bitcast.18, s32[1024]{0:T(1024)S(1)} %pad_clamp_fusion), kind=kCustom, calls=%fused_computation | custom fusion | bytes 524320 | tf_op jit(solution)/shard_map/gather | solution.py:27
  9.4 16.0 %all_to_all.10 = bf16[8,16,1024]{2,1,0:T(8,128)(2,1)S(1)} all-to-all(bf16[8,16,1024]{2,1,0:T(8,128)(2,1)S(1)} %gather_fusion), channel_id=1, replica_groups=mesh['dp'=8,'mp'=4] {'dp'}, dimensions={0} | all-to-all | bytes 524288 | tf_op jit(solution)/shard_map/all_to_all | solution.py:28
  25.4 0.0 copy-done
  25.4 0.9 convolution_bitcast_fusion
  26.3 0.0 all-reduce.2.cloned.1.call-update
  26.3 0.0 copy-start.2
  26.4 30.4 %all-reduce.2.cloned.1.call-done = f32[192,128]{1,0:T(8,128)} async-done(((f32[192,128]{1,0:T(8,128)}), f32[192,128]{1,0:T(8,128)}) %all-reduce.2.cloned.1.call-update) | async-done | bytes 98320 | tf_op jit(solution)/shard_map/psum | solution.py:33
  56.8 0.0 copy-start.1
  56.8 1.1 %reduce_max.9 = f32[192]{0:T(256)S(1)} reduce(f32[192,128]{1,0:T(8,128)} %all-reduce.2.cloned.1.call-done, f32[]{:T(128)} %constant.3.clone.1), dimensions={1}, to_apply=%region_1.0 | reduce | flops 24384 | bytes 99076 | tf_op jit(solution)/shard_map/reduce_max | solution.py:11
  57.9 0.0 copy-done.2
  57.9 0.0 copy-done.1
  57.9 0.2 fusion.2
  58.1 1.2 %fusion.7 = f32[128,1024]{1,0:T(8,128)} fusion(bf16[192,1024]{1,0:T(8,128)(2,1)S(1)} %copy-done, f32[192,128]{1,0:T(8,128)S(1)} %copy-done.1, f32[192]{0:T(256)S(1)} %get-tuple-element.3, s32[192]{0:T(256)S(1)} %copy-done.2, f32[192]{0:T(256)S(1)} %reduce_max.9), kind=kOutput, calls=%fused_computation.16 | convolution fusion | flops 50479104 | bytes 1018112 | tf_op jit(solution)/shard_map/dot_general | solution.py:37
  59.3 5.5 %all-to-all-start.1 = ((f32[8,16,1024]{2,1,0:T(8,128)}), f32[8,16,1024]{2,1,0:T(8,128)S(1)}, u32[]{:S(2)}, u32[]{:S(2)}) async-start(f32[8,16,1024]{2,1,0:T(8,128)} %bitcast.6), calls=%async_computation.1 | async-start | bytes 1048576 | tf_op jit(solution)/shard_map/all_to_all | solution.py:40
  64.8 0.6 subtract_reduce_fusion
  65.4 22.5 %psum.15 = f32[]{:T(128)} all-reduce(f32[]{:T(128)} %subtract_reduce_fusion), channel_id=1, replica_groups=mesh['dp'=8,'mp'=4] {'dp'}, use_global_device_ids=true, to_apply=%region_5.6 | all-reduce | flops 1 | bytes 8 | tf_op jit(solution)/shard_map/psum | solution.py:35
  88.5 1.2 %fusion.8 = f32[192,1024]{1,0:T(8,128)} fusion(bf16[128,1024]{1,0:T(8,128)(2,1)S(1)} %bitcast.17, f32[192,128]{1,0:T(8,128)S(1)} %copy-done.1, f32[192]{0:T(256)S(1)} %get-tuple-element.3, s32[192]{0:T(256)S(1)} %copy-done.2, f32[192]{0:T(256)S(1)} %reduce_max.9), kind=kOutput, calls=%fused_computation.17 | convolution fusion | flops 50479104 | bytes 1149184 | tf_op jit(solution)/shard_map/dot_general | solution.py:36
  89.8 0.0 copy-start.3
  89.8 0.0 all-to-all-done.1
  89.8 0.7 copy-done.3
  90.4 0.7 fusion
  91.1 0.9 copy.11
  (1 shorter events, 0.0 us)
Async XLA Ops:
  7.2 18.2 %copy-start = (bf16[192,1024]{1,0:T(8,128)(2,1)S(1)}, bf16[192,1024]{1,0:T(8,128)(2,1)}, u32[]{:S(2)}) copy-start(bf16[192,1024]{1,0:T(8,128)(2,1)} %param.4) | copy-start | bytes 1179652
  7.2 49.6 %all-reduce.2.cloned.1.call-start = ((), (), s32[]{:S(2)}) async-start(), calls=%async_computation.2 | async-start | bytes 196608 | tf_op jit(solution)/shard_map/psum | solution.py:33
  26.3 31.5 %copy-start.2 = (s32[192]{0:T(256)S(1)}, s32[192]{0:T(256)}, u32[]{:S(2)}) copy-start(s32[192]{0:T(256)} %param.7) | copy-start | bytes 2308
  56.8 1.1 %copy-start.1 = (f32[192,128]{1,0:T(8,128)S(1)}, f32[192,128]{1,0:T(8,128)}, u32[]{:S(2)}) copy-start(f32[192,128]{1,0:T(8,128)} %all-reduce.2.cloned.1.call-done) | copy-start | bytes 294916
  59.3 30.5 %all-to-all-start.1 = ((f32[8,16,1024]{2,1,0:T(8,128)}), f32[8,16,1024]{2,1,0:T(8,128)S(1)}, u32[]{:S(2)}, u32[]{:S(2)}) async-start(f32[8,16,1024]{2,1,0:T(8,128)} %bitcast.6), calls=%async_computation.1 | async-start | bytes 1048576 | tf_op jit(solution)/shard_map/all_to_all | solution.py:40
  89.8 0.7 copy-start.3
Sparse Core Ops, SparseCore 0:
  26.5 30.2 all-reduce.1
where the time goes:
time: 100 us; the launch traced here: 99.9 us
  blocking collectives  38.5 us (38%)
  waiting for transfers between devices  30.4 us (30%)
  between operations  15.9 us (16%)
  starting transfers between devices  5.55 us (6%)
  matrix products  3.96 us (4%)
  local copies, waits for them, and re-layouts  3 us (3%)
  other arithmetic  2.63 us (3%)
    psum x1, waiting for transfers between devices, per_device(): scores = lax.psum(partial_value, 'mp')  30.4 us
    psum x1, blocking collectives, per_device(): loss = lax.psum(loss_sum, 'dp') / (queries.shape[0] * groups)  22.5 us
    all_to_all x1, blocking collectives, per_device(): lax.all_to_all(outgoing, 'dp', split_axis=0, concat_axis=0, tiled=True)  16 us
    all_to_all x1, starting transfers between devices, per_device(): lax.all_to_all(cand_grad.reshape(groups, PBLK, width), 'dp', split_axis=0...  5.52 us
  transfers between devices with their start and end apart: 2, of which 1 were waited for; matrix products, arithmetic and copies ran while one was open for 2% of the time, Pallas kernels for 0%

commit v1 on v0

v1 whole, which is shorter than its diff:
```python
import functools
import jax
import jax.numpy as jnp
from jax import lax
from jax.experimental import pallas as pl
from jax.experimental.pallas import tpu as pltpu
from jax.sharding import PartitionSpec as P

PBLK = 16
PB_DEV = 4
MESH = pl.DeviceIdType.MESH
UNROLL = 8


def flip(index, step, count):
    result, bit = 0, 1
    while bit < count:
        mine, other = (index // bit) % 2, (step // bit) % 2
        result = result + bit * (mine + other - 2 * mine * other)
        bit *= 2
    return result


def each(low, high, body):
    if high - low <= UNROLL:
        for step in range(low, high):
            body(step)
    else:
        lax.fori_loop(low, high, lambda step, carry: (body(step), carry)[1], 0)


def kernel(
    n, m, q_hbm, p_hbm, pair_ref, pos_ref, loss_ref, qgrad_ref, pgrad_ref,
    q, p, outgoing, flat, part, shares, weights, turned, hits,
    sent_wide, sent_slim, got_wide, got_slim, loss_mp, loss_dp,
    local_sem, a_send, a_recv, b_send, b_recv, c_send, c_recv,
    d_send, d_recv, e_send, e_recv, f_send, f_recv,
):
    half = n // 2
    rows = q.shape[0]
    share = rows // m
    me = lax.axis_index("dp")
    mine = lax.axis_index("mp")

    def remote(src, dst, send, recv, device):
        return pltpu.make_async_remote_copy(
            src_ref=src, dst_ref=dst, send_sem=send, recv_sem=recv,
            device_id=device, device_id_type=MESH,
        )

    def across(step):
        return (flip(me, step, n), mine)

    def beside(step):
        return (me, flip(mine, step, m))

    load_p = pltpu.make_async_copy(p_hbm, p, local_sem.at[0])
    load_q = pltpu.make_async_copy(q_hbm, q, local_sem.at[1])
    load_p.start()
    load_q.start()
    barrier = pltpu.get_barrier_semaphore()

    def greet(step):
        pl.semaphore_signal(barrier, inc=1, device_id=across(step), device_id_type=MESH)

    each(1, n, greet)
    for step in range(1, m):
        pl.semaphore_signal(barrier, inc=1, device_id=beside(step), device_id_type=MESH)

    def slot(step):
        return pl.ds(step * PBLK, PBLK)

    def chosen(step):
        return p[pair_ref[flip(me, step, n), 0]]

    load_p.wait()

    def pack(step):
        outgoing[step] = chosen(step)

    each(1, n, pack)
    flat[0:PBLK, :] = chosen(0)
    pl.semaphore_wait(barrier, n - 1 + m - 1)

    def passage(step):
        return remote(
            outgoing.at[step], flat.at[slot(step)], a_send.at[step], a_recv.at[step], across(step)
        )

    each(half, n, lambda step: passage(step).start())
    each(1, half, lambda step: passage(step).start())

    lanes = lax.broadcasted_iota(jnp.int32, (1, n * PBLK), 1)
    first = pl.multiple_of(mine * share, share)

    def mark(row):
        spot = pos_ref[first + row] ^ (me * PBLK)
        hits[pl.ds(row, 1), :] = (lanes == spot).astype(jnp.float32)

    for row in range(share):
        mark(row)
    load_q.wait()
    each(1, n, lambda step: passage(step).wait_recv())

    part[...] = lax.dot_general(
        q[...], flat[...], (((1,), (1,)), ((), ())), preferred_element_type=jnp.float32
    )

    def their_rows(step):
        return pl.ds(pl.multiple_of(flip(mine, step, m) * share, share), share)

    def score(step):
        return remote(
            part.at[their_rows(step)], shares.at[step], b_send.at[step], b_recv.at[step],
            beside(step),
        )

    for step in reversed(range(1, m)):
        score(step).start()
    scores = part[pl.ds(first, share), :]
    for step in range(1, m):
        score(step).wait_recv()
        scores = scores + shares[step]
    top = jnp.max(scores, axis=1, keepdims=True)
    shifted = jnp.exp(scores - top)
    total = jnp.sum(shifted, axis=1, keepdims=True)
    hit = hits[...]
    weights[pl.ds(first, share), :] = (shifted / total - hit).astype(jnp.bfloat16)

    def weight(step):
        place = pl.ds(first, share)
        return remote(
            weights.at[place], weights.at[place], c_send.at[step], c_recv.at[step], beside(step)
        )

    def arriving(step):
        place = their_rows(step)
        return remote(
            weights.at[place], weights.at[place], c_send.at[step], c_recv.at[step], beside(step)
        )

    for step in reversed(range(1, m)):
        weight(step).start()

    positive = jnp.sum(hit * scores, axis=1, keepdims=True)
    losses = top + jnp.log(total) - positive
    loss_mp[0] = jnp.broadcast_to(jnp.sum(losses, axis=0, keepdims=True), loss_mp.shape[1:])

    def loss_beside(step):
        return remote(
            loss_mp.at[0], loss_mp.at[step], d_send.at[step], d_recv.at[step], beside(step)
        )

    for step in range(1, m):
        loss_beside(step).start()
    for step in range(1, m):
        arriving(step).wait_recv()
    turned[...] = weights[...].astype(jnp.float32).T.astype(jnp.bfloat16)

    def slim(step):
        return remote(
            sent_slim.at[step - half], got_slim.at[step - half], e_send.at[step], e_recv.at[step],
            across(step),
        )

    def wide(step):
        return remote(
            sent_wide.at[step], got_wide.at[step], e_send.at[step], e_recv.at[step], across(step)
        )

    group = min(half, 4)

    def grads(index):
        block = turned[pl.ds(index * group * PBLK, group * PBLK), :]
        result = jnp.dot(block, q[...], preferred_element_type=jnp.float32)
        return result.reshape(group, PBLK, q.shape[1])

    def give_slim(index):
        sent_slim[pl.ds(index * group - half, group)] = grads(index).astype(jnp.bfloat16)
        for place in range(group):
            slim(index * group + place).start()

    def give_wide(index):
        sent_wide[pl.ds(index * group, group)] = grads(index)
        for place in range(group):
            step = index * group + place
            if isinstance(step, int):
                if step:
                    wide(step).start()
            else:
                pl.when(step > 0)(lambda step=step: wide(step).start())

    each(half // group, n // group, give_slim)
    each(0, half // group, give_wide)

    for step in range(1, m):
        loss_beside(step).wait_recv()
    loss_dp[0] = jnp.sum(loss_mp[...], axis=0)

    def loss_across(step):
        return remote(
            loss_dp.at[0], loss_dp.at[step], f_send.at[step], f_recv.at[step], across(step)
        )

    each(1, n, lambda step: loss_across(step).start())

    qgrad_ref[...] = jnp.dot(weights[...], flat[...], preferred_element_type=jnp.float32)

    pgrad_ref[...] = jnp.zeros_like(pgrad_ref)

    def collect(step, block):
        pick = jnp.full(block.shape, pair_ref[flip(me, step, n), 0], jnp.int32)
        for place in range(PB_DEV):
            pgrad_ref[pl.ds(place * PBLK, PBLK), :] += jnp.where(pick == place, block, 0.0)

    def take_wide(step):
        wide(step).wait_recv()
        collect(step, got_wide[step])

    def take_slim(step):
        slim(step).wait_recv()
        collect(step, got_slim[step - half].astype(jnp.float32))

    collect(0, sent_wide[0])
    each(1, half, take_wide)
    each(half, n, take_slim)
    each(1, n, lambda step: loss_across(step).wait_recv())
    loss_ref[...] = jnp.sum(loss_dp[...], axis=0)[0:1, 0:1] / (rows * n)

    def settle(step):
        passage(step).wait_send()
        loss_across(step).wait_send()

    each(1, n, settle)
    each(1, half, lambda step: wide(step).wait_send())
    each(half, n, lambda step: slim(step).wait_send())
    for step in range(1, m):
        score(step).wait_send()
        weight(step).wait_send()
        loss_beside(step).wait_send()


def per_device(n, m, queries, passages, pair_block, positives):
    rows, width = queries.shape
    half, share, cands = n // 2, rows // m, n * PBLK
    vmem, sems = pltpu.VMEM, pltpu.SemaphoreType.DMA
    bf16, f32 = jnp.bfloat16, jnp.float32
    scratch = [
        vmem((rows, width), bf16),
        vmem((PB_DEV, PBLK, width), bf16),
        vmem((n, PBLK, width), bf16),
        vmem((cands, width), bf16),
        vmem((rows, cands), f32),
        vmem((m, share, cands), f32),
        vmem((rows, cands), bf16),
        vmem((cands, rows), bf16),
        vmem((share, cands), f32),
        vmem((half, PBLK, width), f32),
        vmem((half, PBLK, width), bf16),
        vmem((half, PBLK, width), f32),
        vmem((half, PBLK, width), bf16),
        vmem((m, 8, 128), f32),
        vmem((n, 8, 128), f32),
        sems((2,)),
        sems((n,)), sems((n,)), sems((m,)), sems((m,)), sems((m,)), sems((m,)),
        sems((m,)), sems((m,)), sems((n,)), sems((n,)), sems((n,)), sems((n,)),
    ]
    anywhere = pl.BlockSpec(memory_space=pl.ANY)
    smem = pl.BlockSpec(memory_space=pltpu.SMEM)
    inside = pl.BlockSpec(memory_space=pltpu.VMEM)
    loss, query_grad, passage_grad = pl.pallas_call(
        functools.partial(kernel, n, m),
        out_shape=[
            jax.ShapeDtypeStruct((1, 1), f32),
            jax.ShapeDtypeStruct((rows, width), f32),
            jax.ShapeDtypeStruct(passages.shape, f32),
        ],
        in_specs=[anywhere, anywhere, smem, smem],
        out_specs=[inside, inside, inside],
        scratch_shapes=scratch,
        compiler_params=pltpu.CompilerParams(
            collective_id=0, has_side_effects=True,
            vmem_limit_bytes=(16 if n <= 16 else 56) << 20,
        ),
    )(queries, passages.reshape(PB_DEV, PBLK, width), pair_block, positives)
    return loss.reshape(()), query_grad, passage_grad


def solution(mesh):
    n, m = mesh.shape["dp"], mesh.shape["mp"]
    in_specs = (P("dp", "mp"), P("dp", "mp"), P(None, "dp"), P("dp"))
    out_specs = (P(), P("dp", "mp"), P("dp", "mp"))
    return jax.shard_map(
        functools.partial(per_device, n, m),
        mesh=mesh, in_specs=in_specs, out_specs=out_specs, check_vma=False,
    )
```

time: 100 us -> 38.3 us (0.38)
  blocking collectives: 38.5 us -> 0 us
  Pallas kernels: 0 us -> 30.9 us
  waiting for transfers between devices: 30.4 us -> 0 us
  between operations: 15.9 us -> 2.4 us
  starting transfers between devices: 5.55 us -> 0 us
  matrix products: 3.96 us -> 0 us
  other arithmetic: 2.63 us -> 0 us
  local copies, waits for them, and re-layouts: 3 us -> 4.81 us
    pallas_call x0 -> x1, Pallas kernels: none -> 30.9 us  [per_device(): pl.pallas_call(functools.partial(kernel, n, m), out_shape=[jax.ShapeDtype...]
    psum x1 -> x0, waiting for transfers between devices: 30.4 us -> none  [per_device(): scores = lax.psum(partial_value, 'mp')]
    psum x1 -> x0, blocking collectives: 22.5 us -> none  [per_device(): loss = lax.psum(loss_sum, 'dp') / (queries.shape[0] * groups)]
    all_to_all x1 -> x0, blocking collectives: 16 us -> none  [per_device(): lax.all_to_all(outgoing, 'dp', split_axis=0, concat_axis=0, tiled=True)]
    all_to_all x1 -> x0, starting transfers between devices: 5.52 us -> none  [per_device(): lax.all_to_all(cand_grad.reshape(groups, PBLK, width), 'dp', split_axis=0...]
    unnamed x8 -> x11, local copies, waits for them, and re-layouts: 0.67 us -> 4.81 us
    dot_general x4 -> x0, matrix products: 3.96 us -> none  [the longest x1 1.22 us: per_device(): query_grad = jnp.dot(weights, flat, preferred_element_type=jnp.float32)]
    gather x1 -> x0, local copies, waits for them, and re-layouts: 1.47 us -> none  [per_device(): outgoing = owned[picked]]
  transfers between devices with their start and end apart: 2 -> 0, of which waited for: 1 -> 0; matrix products, arithmetic and copies ran while one was open for 2% -> 0% of each run, Pallas kernels for 0% -> 0%
where the time goes in v1:
time: 38.3 us; the launch traced here: 38.1 us
  Pallas kernels  30.9 us (81%)
  local copies, waits for them, and re-layouts  4.81 us (13%)
  between operations  2.4 us (6%)
    pallas_call x1, Pallas kernels, per_device(): pl.pallas_call(functools.partial(kernel, n, m), out_shape=[jax.ShapeDtype...  30.9 us
    unnamed x11, local copies, waits for them, and re-layouts  4.81 us

profile of v1, /device:TPU:0, one launch (start us, length us, event | category | flops | bytes accessed | tf_op | source)
XLA Modules:
  0.0 38.1 jit_solution(6771912485143718792)
XLA Ops:
  0.6 0.0 copy-start.3
  0.6 0.6 %copy-done.3 = s32[8,1]{0,1:T(1,128)S(1)} copy-done((s32[8,1]{0,1:T(1,128)S(1)}, s32[8,1]{0,1:T(1,128)}, u32[]{:S(2)}) %copy-start.3) | copy-done | bytes 56
  1.3 0.0 copy-start.2
  1.3 0.1 copy.7.pair_ref
  1.4 0.6 %copy-done.2 = s32[192]{0:T(256)S(1)} copy-done((s32[192]{0:T(256)S(1)}, s32[192]{0:T(256)}, u32[]{:S(2)}) %copy-start.2) | copy-done | bytes 792
  2.0 0.0 copy-start
  2.0 1.0 %copy-done = bf16[192,1024]{1,0:T(8,128)(2,1)S(1)} copy-done((bf16[192,1024]{1,0:T(8,128)(2,1)S(1)}, bf16[192,1024]{1,0:T(8,128)(2,1)}, u32[]{:S(2)}) %copy-start) | copy-done | bytes 393240
  3.0 0.0 copy-start.1
  3.0 0.9 %copy-done.1 = bf16[64,1024]{1,0:T(8,128)(2,1)S(1)} copy-done((bf16[64,1024]{1,0:T(8,128)(2,1)S(1)}, bf16[64,1024]{1,0:T(8,128)(2,1)}, u32[]{:S(2)}) %copy-start.1) | copy-done | bytes 131096
  3.9 30.9 %shard_map.67 = (f32[1,1]{1,0:T(1,128)}, f32[192,1024]{1,0:T(8,128)S(1)}, f32[64,1024]{1,0:T(8,128)S(1)}) custom-call(bf16[192,1024]{1,0:T(8,128)(2,1)S(1)} %copy-done, bf16[4,16,1024]{2,1,0:T(8,128)(2,1)S(1)} %bitcast.2, s32[8,1]{1,0:T(8,128)S(1)} %copy.7.pair_ref, s32[192]{0:T(256)S(1)} %copy-done.2), custom_call_target="tpu_custom_call" | custom-call | tf_op jit(solution)/shard_map/pallas_call | solution.py:271
  35.3 0.9 %copy.12 = f32[192,1024]{1,0:T(8,128)} copy(f32[192,1024]{1,0:T(8,128)S(1)} %get-tuple-element.13) | data formatting | bytes 1572864
  36.2 0.7 %copy.13 = f32[64,1024]{1,0:T(8,128)} copy(f32[64,1024]{1,0:T(8,128)S(1)} %get-tuple-element.14) | data formatting | bytes 524288
Async XLA Ops:
  0.6 0.7 %copy-start.3 = (s32[8,1]{0,1:T(1,128)S(1)}, s32[8,1]{0,1:T(1,128)}, u32[]{:S(2)}) copy-start(s32[8,1]{0,1:T(1,128)} %param.6) | copy-start | bytes 100
  1.3 0.7 %copy-start.2 = (s32[192]{0:T(256)S(1)}, s32[192]{0:T(256)}, u32[]{:S(2)}) copy-start(s32[192]{0:T(256)} %pos_ref.1) | copy-start | bytes 2308
  2.0 1.0 %copy-start = (bf16[192,1024]{1,0:T(8,128)(2,1)S(1)}, bf16[192,1024]{1,0:T(8,128)(2,1)}, u32[]{:S(2)}) copy-start(bf16[192,1024]{1,0:T(8,128)(2,1)} %q_hbm.1) | copy-start | bytes 1179652
  3.0 0.9 %copy-start.1 = (bf16[64,1024]{1,0:T(8,128)(2,1)S(1)}, bf16[64,1024]{1,0:T(8,128)(2,1)}, u32[]{:S(2)}) copy-start(bf16[64,1024]{1,0:T(8,128)(2,1)} %param.5) | copy-start | bytes 393220

commit v2 on v1

--- a/solution.py
+++ b/solution.py
@@ -30,8 +30,8 @@
 
 
 def kernel(
-    n, m, q_hbm, p_hbm, pair_ref, pos_ref, loss_ref, qgrad_ref, pgrad_ref,
-    q, p, outgoing, flat, part, shares, weights, turned, hits,
+    n, m, q_hbm, p_hbm, pair_ref, pos_ref, loss_hbm, qgrad_hbm, pgrad_hbm,
+    loss_ref, qgrad_ref, pgrad_ref, q, p, outgoing, flat, part, shares, weights, turned, hits,
     sent_wide, sent_slim, got_wide, got_slim, loss_mp, loss_dp,
     local_sem, a_send, a_recv, b_send, b_recv, c_send, c_recv,
     d_send, d_recv, e_send, e_recv, f_send, f_recv,
@@ -71,7 +71,7 @@
         return pl.ds(step * PBLK, PBLK)
 
     def chosen(step):
-        return p[pair_ref[flip(me, step, n), 0]]
+        return p[pair_ref[flip(me, step, n)]]
 
     load_p.wait()
 
@@ -205,11 +205,13 @@
     each(1, n, lambda step: loss_across(step).start())
 
     qgrad_ref[...] = jnp.dot(weights[...], flat[...], preferred_element_type=jnp.float32)
+    save_q = pltpu.make_async_copy(qgrad_ref, qgrad_hbm, local_sem.at[2])
+    save_q.start()
 
     pgrad_ref[...] = jnp.zeros_like(pgrad_ref)
 
     def collect(step, block):
-        pick = jnp.full(block.shape, pair_ref[flip(me, step, n), 0], jnp.int32)
+        pick = jnp.full(block.shape, pair_ref[flip(me, step, n)], jnp.int32)
         for place in range(PB_DEV):
             pgrad_ref[pl.ds(place * PBLK, PBLK), :] += jnp.where(pick == place, block, 0.0)
 
@@ -224,8 +226,12 @@
     collect(0, sent_wide[0])
     each(1, half, take_wide)
     each(half, n, take_slim)
+    save_p = pltpu.make_async_copy(pgrad_ref, pgrad_hbm, local_sem.at[3])
+    save_p.start()
     each(1, n, lambda step: loss_across(step).wait_recv())
     loss_ref[...] = jnp.sum(loss_dp[...], axis=0)[0:1, 0:1] / (rows * n)
+    save_loss = pltpu.make_async_copy(loss_ref, loss_hbm, local_sem.at[4])
+    save_loss.start()
 
     def settle(step):
         passage(step).wait_send()
@@ -238,6 +244,22 @@
         score(step).wait_send()
         weight(step).wait_send()
         loss_beside(step).wait_send()
+    save_q.wait()
+    save_p.wait()
+    save_loss.wait()
+
+
+def hand_over(*refs):
+    sems = refs[-1]
+    count = len(refs) // 2
+    copies = [
+        pltpu.make_async_copy(refs[place], refs[count + place], sems.at[place])
+        for place in range(count)
+    ]
+    for copy in copies:
+        copy.start()
+    for copy in copies:
+        copy.wait()
 
 
 def per_device(n, m, queries, passages, pair_block, positives):
@@ -245,7 +267,15 @@
     half, share, cands = n // 2, rows // m, n * PBLK
     vmem, sems = pltpu.VMEM, pltpu.SemaphoreType.DMA
     bf16, f32 = jnp.bfloat16, jnp.float32
+    results = [
+        jax.ShapeDtypeStruct((1, 1), f32),
+        jax.ShapeDtypeStruct((rows, width), f32),
+        jax.ShapeDtypeStruct(passages.shape, f32),
+    ]
     scratch = [
+        vmem((1, 1), f32),
+        vmem((rows, width), f32),
+        vmem(passages.shape, f32),
         vmem((rows, width), bf16),
         vmem((PB_DEV, PBLK, width), bf16),
         vmem((n, PBLK, width), bf16),
@@ -261,28 +291,30 @@
         vmem((half, PBLK, width), bf16),
         vmem((m, 8, 128), f32),
         vmem((n, 8, 128), f32),
-        sems((2,)),
+        sems((5,)),
         sems((n,)), sems((n,)), sems((m,)), sems((m,)), sems((m,)), sems((m,)),
         sems((m,)), sems((m,)), sems((n,)), sems((n,)), sems((n,)), sems((n,)),
     ]
     anywhere = pl.BlockSpec(memory_space=pl.ANY)
     smem = pl.BlockSpec(memory_space=pltpu.SMEM)
-    inside = pl.BlockSpec(memory_space=pltpu.VMEM)
-    loss, query_grad, passage_grad = pl.pallas_call(
+    found = pl.pallas_call(
         functools.partial(kernel, n, m),
-        out_shape=[
-            jax.ShapeDtypeStruct((1, 1), f32),
-            jax.ShapeDtypeStruct((rows, width), f32),
-            jax.ShapeDtypeStruct(passages.shape, f32),
-        ],
+        out_shape=results,
         in_specs=[anywhere, anywhere, smem, smem],
-        out_specs=[inside, inside, inside],
+        out_specs=[anywhere] * 3,
         scratch_shapes=scratch,
         compiler_params=pltpu.CompilerParams(
-            collective_id=0, has_side_effects=True,
-            vmem_limit_bytes=(16 if n <= 16 else 56) << 20,
+            collective_id=0, has_side_effects=True, vmem_limit_bytes=60 << 20,
         ),
-    )(queries, passages.reshape(PB_DEV, PBLK, width), pair_block, positives)
+    )(queries, passages.reshape(PB_DEV, PBLK, width), pair_block.reshape(n), positives)
+    loss, query_grad, passage_grad = pl.pallas_call(
+        hand_over,
+        out_shape=results,
+        in_specs=[anywhere] * 3,
+        out_specs=[anywhere] * 3,
+        scratch_shapes=[sems((3,))],
+        compiler_params=pltpu.CompilerParams(vmem_limit_bytes=60 << 20),
+    )(*found)
     return loss.reshape(()), query_grad, passage_grad
 
 

time: 38.3 us -> 64.9 us (1.69)
  Pallas kernels: 30.9 us -> 64.1 us
  local copies, waits for them, and re-layouts: 4.81 us -> 0 us
  between operations: 2.4 us -> 0.64 us
    pallas_call x1 -> x2, Pallas kernels: 30.9 us -> 64.1 us  [the longest x1 33.5 us: per_device(): pl.pallas_call(hand_over, out_shape=results, in_specs=[anywhere] * 3, out...]
    unnamed x11 -> x0, local copies, waits for them, and re-layouts: 4.81 us -> none
where the time goes in v2:
time: 64.9 us; the launch traced here: 64.7 us
  Pallas kernels  64.1 us (99%)
    pallas_call x1, Pallas kernels, per_device(): pl.pallas_call(hand_over, out_shape=results, in_specs=[anywhere] * 3, out...  33.5 us
    pallas_call x1, Pallas kernels, per_device(): pl.pallas_call(functools.partial(kernel, n, m), out_shape=results, in_spe...  30.6 us

profile of v2, /device:TPU:0, one launch (start us, length us, event | category | flops | bytes accessed | tf_op | source)
XLA Modules:
  0.0 64.7 jit_solution(11108967013402931227)
XLA Ops:
  0.6 30.6 %shard_map.67 = (f32[1,1]{1,0:T(1,128)}, f32[192,1024]{1,0:T(8,128)}, f32[64,1024]{1,0:T(8,128)}) custom-call(bf16[192,1024]{1,0:T(8,128)(2,1)} %q_hbm.1, bf16[4,16,1024]{2,1,0:T(8,128)(2,1)} %bitcast.3, s32[8]{0:T(128)} %bitcast.4, s32[192]{0:T(256)} %pos_ref.1), custom_call_target="tpu_custom_call" | custom-call | tf_op jit(solution)/shard_map/pallas_call | solution.py:300
  31.2 33.5 %shard_map.68 = (f32[1,1]{1,0:T(1,128)}, f32[192,1024]{1,0:T(8,128)}, f32[64,1024]{1,0:T(8,128)}) custom-call(f32[1,1]{1,0:T(1,128)} %get-tuple-element.9.refs_0_, f32[192,1024]{1,0:T(8,128)} %get-tuple-element.10.refs_1_, f32[64,1024]{1,0:T(8,128)} %get-tuple-element.11.refs_2_), custom_call_target="tpu_custom_call" | custom-call | tf_op jit(solution)/shard_map/pallas_call | solution.py:310

commit v3 on v2

--- a/solution.py
+++ b/solution.py
@@ -30,8 +30,8 @@
 
 
 def kernel(
-    n, m, q_hbm, p_hbm, pair_ref, pos_ref, loss_hbm, qgrad_hbm, pgrad_hbm,
-    loss_ref, qgrad_ref, pgrad_ref, q, p, outgoing, flat, part, shares, weights, turned, hits,
+    n, m, q_hbm, p_hbm, pair_hbm, pos_hbm, loss_hbm, qgrad_hbm, pgrad_hbm,
+    loss_ref, qgrad_ref, pgrad_ref, pair_ref, pos_ref, q, p, outgoing, flat, part, shares, weights, turned, hits,
     sent_wide, sent_slim, got_wide, got_slim, loss_mp, loss_dp,
     local_sem, a_send, a_recv, b_send, b_recv, c_send, c_recv,
     d_send, d_recv, e_send, e_recv, f_send, f_recv,
@@ -56,7 +56,11 @@
 
     load_p = pltpu.make_async_copy(p_hbm, p, local_sem.at[0])
     load_q = pltpu.make_async_copy(q_hbm, q, local_sem.at[1])
+    load_pair = pltpu.make_async_copy(pair_hbm, pair_ref, local_sem.at[2])
+    load_pos = pltpu.make_async_copy(pos_hbm, pos_ref, local_sem.at[3])
+    load_pair.start()
     load_p.start()
+    load_pos.start()
     load_q.start()
     barrier = pltpu.get_barrier_semaphore()
 
@@ -73,6 +77,7 @@
     def chosen(step):
         return p[pair_ref[flip(me, step, n)]]
 
+    load_pair.wait()
     load_p.wait()
 
     def pack(step):
@@ -97,6 +102,7 @@
         spot = pos_ref[first + row] ^ (me * PBLK)
         hits[pl.ds(row, 1), :] = (lanes == spot).astype(jnp.float32)
 
+    load_pos.wait()
     for row in range(share):
         mark(row)
     load_q.wait()
@@ -205,7 +211,7 @@
     each(1, n, lambda step: loss_across(step).start())
 
     qgrad_ref[...] = jnp.dot(weights[...], flat[...], preferred_element_type=jnp.float32)
-    save_q = pltpu.make_async_copy(qgrad_ref, qgrad_hbm, local_sem.at[2])
+    save_q = pltpu.make_async_copy(qgrad_ref, qgrad_hbm, local_sem.at[4])
     save_q.start()
 
     pgrad_ref[...] = jnp.zeros_like(pgrad_ref)
@@ -226,11 +232,11 @@
     collect(0, sent_wide[0])
     each(1, half, take_wide)
     each(half, n, take_slim)
-    save_p = pltpu.make_async_copy(pgrad_ref, pgrad_hbm, local_sem.at[3])
+    save_p = pltpu.make_async_copy(pgrad_ref, pgrad_hbm, local_sem.at[5])
     save_p.start()
     each(1, n, lambda step: loss_across(step).wait_recv())
     loss_ref[...] = jnp.sum(loss_dp[...], axis=0)[0:1, 0:1] / (rows * n)
-    save_loss = pltpu.make_async_copy(loss_ref, loss_hbm, local_sem.at[4])
+    save_loss = pltpu.make_async_copy(loss_ref, loss_hbm, local_sem.at[6])
     save_loss.start()
 
     def settle(step):
@@ -249,17 +255,24 @@
     save_loss.wait()
 
 
-def hand_over(*refs):
-    sems = refs[-1]
-    count = len(refs) // 2
-    copies = [
-        pltpu.make_async_copy(refs[place], refs[count + place], sems.at[place])
-        for place in range(count)
-    ]
-    for copy in copies:
-        copy.start()
-    for copy in copies:
-        copy.wait()
+def hand_over(loss_in, qgrad_in, pgrad_in, loss_out, qgrad_out, pgrad_out, loss, qgrad, pgrad, sems):
+    parts = [(loss_in, loss, loss_out)]
+    piece = 64
+    for source, held, target in ((qgrad_in, qgrad, qgrad_out), (pgrad_in, pgrad, pgrad_out)):
+        for start in range(0, held.shape[0], piece):
+            place = pl.ds(start, piece)
+            parts.append((source.at[place], held.at[place], target.at[place]))
+    loads, stores = [], []
+    for index, (source, held, target) in enumerate(parts):
+        loads.append(pltpu.make_async_copy(source, held, sems.at[0, index]))
+        stores.append(pltpu.make_async_copy(held, target, sems.at[1, index]))
+    for load in loads:
+        load.start()
+    for load, store in zip(loads, stores):
+        load.wait()
+        store.start()
+    for store in stores:
+        store.wait()
 
 
 def per_device(n, m, queries, passages, pair_block, positives):
@@ -272,10 +285,10 @@
         jax.ShapeDtypeStruct((rows, width), f32),
         jax.ShapeDtypeStruct(passages.shape, f32),
     ]
-    scratch = [
-        vmem((1, 1), f32),
-        vmem((rows, width), f32),
-        vmem(passages.shape, f32),
+    held = [vmem((1, 1), f32), vmem((rows, width), f32), vmem(passages.shape, f32)]
+    scratch = held + [
+        pltpu.SMEM((n,), jnp.int32),
+        pltpu.SMEM((rows,), jnp.int32),
         vmem((rows, width), bf16),
         vmem((PB_DEV, PBLK, width), bf16),
         vmem((n, PBLK, width), bf16),
@@ -291,20 +304,20 @@
         vmem((half, PBLK, width), bf16),
         vmem((m, 8, 128), f32),
         vmem((n, 8, 128), f32),
-        sems((5,)),
+        sems((7,)),
         sems((n,)), sems((n,)), sems((m,)), sems((m,)), sems((m,)), sems((m,)),
         sems((m,)), sems((m,)), sems((n,)), sems((n,)), sems((n,)), sems((n,)),
     ]
     anywhere = pl.BlockSpec(memory_space=pl.ANY)
-    smem = pl.BlockSpec(memory_space=pltpu.SMEM)
     found = pl.pallas_call(
         functools.partial(kernel, n, m),
         out_shape=results,
-        in_specs=[anywhere, anywhere, smem, smem],
+        in_specs=[anywhere] * 4,
         out_specs=[anywhere] * 3,
         scratch_shapes=scratch,
         compiler_params=pltpu.CompilerParams(
-            collective_id=0, has_side_effects=True, vmem_limit_bytes=60 << 20,
+            collective_id=0, has_side_effects=True,
+            vmem_limit_bytes=60 << 20,
         ),
     )(queries, passages.reshape(PB_DEV, PBLK, width), pair_block.reshape(n), positives)
     loss, query_grad, passage_grad = pl.pallas_call(
@@ -312,7 +325,7 @@
         out_shape=results,
         in_specs=[anywhere] * 3,
         out_specs=[anywhere] * 3,
-        scratch_shapes=[sems((3,))],
+        scratch_shapes=held + [sems((2, 1 + (rows + passages.shape[0]) // 64))],
         compiler_params=pltpu.CompilerParams(vmem_limit_bytes=60 << 20),
     )(*found)
     return loss.reshape(()), query_grad, passage_grad

time: 64.9 us -> 33.3 us (0.51)
  Pallas kernels: 64.1 us -> 32.5 us
    pallas_call x1, Pallas kernels: 33.5 us -> 2.64 us  [per_device(): pl.pallas_call(hand_over, out_shape=results, in_specs=[anywhere] * 3, out...]
    pallas_call x1, Pallas kernels: 30.6 us -> 29.9 us  [per_device(): pl.pallas_call(functools.partial(kernel, n, m), out_shape=results, in_spe...]
where the time goes in v3:
time: 33.3 us; the launch traced here: 33.2 us
  Pallas kernels  32.5 us (98%)
  between operations  0.64 us (2%)
    pallas_call x1, Pallas kernels, per_device(): pl.pallas_call(functools.partial(kernel, n, m), out_shape=results, in_spe...  29.9 us
    pallas_call x1, Pallas kernels, per_device(): pl.pallas_call(hand_over, out_shape=results, in_specs=[anywhere] * 3, out...  2.64 us

profile of v3, /device:TPU:0, one launch (start us, length us, event | category | flops | bytes accessed | tf_op | source)
XLA Modules:
  0.0 33.2 jit_solution(11231342231650996588)
XLA Ops:
  0.6 29.9 %shard_map.67 = (f32[1,1]{1,0:T(1,128)}, f32[192,1024]{1,0:T(8,128)}, f32[64,1024]{1,0:T(8,128)}) custom-call(bf16[192,1024]{1,0:T(8,128)(2,1)} %q_hbm.1, bf16[4,16,1024]{2,1,0:T(8,128)(2,1)} %bitcast.3, s32[8]{0:T(128)} %bitcast.4, s32[192]{0:T(256)} %pos_hbm.1), custom_call_target="tpu_custom_call" | custom-call | tf_op jit(solution)/shard_map/pallas_call | solution.py:312
  30.5 2.6 %shard_map.68 = (f32[1,1]{1,0:T(1,128)}, f32[192,1024]{1,0:T(8,128)}, f32[64,1024]{1,0:T(8,128)}) custom-call(f32[1,1]{1,0:T(1,128)} %get-tuple-element.9.loss_in, f32[192,1024]{1,0:T(8,128)} %get-tuple-element.10.qgrad_in, f32[64,1024]{1,0:T(8,128)} %get-tuple-element.11.pgrad_in), custom_call_target="tpu_custom_call" | custom-call | tf_op jit(solution)/shard_map/pallas_call | solution.py:323

commit v4 on v3

--- a/solution.py
+++ b/solution.py
@@ -10,6 +10,7 @@
 PB_DEV = 4
 MESH = pl.DeviceIdType.MESH
 UNROLL = 8
+LANES = 128
 
 
 def flip(index, step, count):
@@ -31,14 +32,12 @@
 
 def kernel(
     n, m, q_hbm, p_hbm, pair_hbm, pos_hbm, loss_hbm, qgrad_hbm, pgrad_hbm,
-    loss_ref, qgrad_ref, pgrad_ref, pair_ref, pos_ref, q, p, outgoing, flat, part, shares, weights, turned, hits,
-    sent_wide, sent_slim, got_wide, got_slim, loss_mp, loss_dp,
-    local_sem, a_send, a_recv, b_send, b_recv, c_send, c_recv,
-    d_send, d_recv, e_send, e_recv, f_send, f_recv,
+    loss_ref, qgrad_ref, pgrad_ref, pair_ref, pos_ref, q, p, outgoing, flat, part, shares, turned,
+    sent_wide, sent_slim, got_wide, got_slim, loss_dp,
+    local_sem, a_send, a_recv, b_send, b_recv, e_send, e_recv, f_send, f_recv,
 ):
     half = n // 2
     rows = q.shape[0]
-    share = rows // m
     me = lax.axis_index("dp")
     mine = lax.axis_index("mp")
 
@@ -95,73 +94,88 @@
     each(half, n, lambda step: passage(step).start())
     each(1, half, lambda step: passage(step).start())
 
-    lanes = lax.broadcasted_iota(jnp.int32, (1, n * PBLK), 1)
-    first = pl.multiple_of(mine * share, share)
-
-    def mark(row):
-        spot = pos_ref[first + row] ^ (me * PBLK)
-        hits[pl.ds(row, 1), :] = (lanes == spot).astype(jnp.float32)
-
     load_pos.wait()
-    for row in range(share):
-        mark(row)
     load_q.wait()
-    each(1, n, lambda step: passage(step).wait_recv())
-
-    part[...] = lax.dot_general(
-        q[...], flat[...], (((1,), (1,)), ((), ())), preferred_element_type=jnp.float32
-    )
-
-    def their_rows(step):
-        return pl.ds(pl.multiple_of(flip(mine, step, m) * share, share), share)
-
-    def score(step):
-        return remote(
-            part.at[their_rows(step)], shares.at[step], b_send.at[step], b_recv.at[step],
-            beside(step),
-        )
-
-    for step in reversed(range(1, m)):
-        score(step).start()
-    scores = part[pl.ds(first, share), :]
-    for step in range(1, m):
-        score(step).wait_recv()
-        scores = scores + shares[step]
-    top = jnp.max(scores, axis=1, keepdims=True)
-    shifted = jnp.exp(scores - top)
-    total = jnp.sum(shifted, axis=1, keepdims=True)
-    hit = hits[...]
-    weights[pl.ds(first, share), :] = (shifted / total - hit).astype(jnp.bfloat16)
-
-    def weight(step):
-        place = pl.ds(first, share)
-        return remote(
-            weights.at[place], weights.at[place], c_send.at[step], c_recv.at[step], beside(step)
-        )
-
-    def arriving(step):
-        place = their_rows(step)
-        return remote(
-            weights.at[place], weights.at[place], c_send.at[step], c_recv.at[step], beside(step)
-        )
-
-    for step in reversed(range(1, m)):
-        weight(step).start()
-
-    positive = jnp.sum(hit * scores, axis=1, keepdims=True)
-    losses = top + jnp.log(total) - positive
-    loss_mp[0] = jnp.broadcast_to(jnp.sum(losses, axis=0, keepdims=True), loss_mp.shape[1:])
-
-    def loss_beside(step):
-        return remote(
-            loss_mp.at[0], loss_mp.at[step], d_send.at[step], d_recv.at[step], beside(step)
-        )
-
-    for step in range(1, m):
-        loss_beside(step).start()
-    for step in range(1, m):
-        arriving(step).wait_recv()
-    turned[...] = weights[...].astype(jnp.float32).T.astype(jnp.bfloat16)
+
+    chunks = ((0, half), (half, half + n // 4), (half + n // 4, n))
+
+    def packed(index):
+        low, high = chunks[index]
+        size = (high - low) * PBLK
+        return pl.ds(low * PBLK * 3 // 2, size * 3 // 2), size
+
+    def score(index, step):
+        place, _ = packed(index)
+        return remote(
+            part.at[place], shares.at[step, place], b_send.at[index, step],
+            b_recv.at[index, step], beside(step),
+        )
+
+    for index, (low, high) in enumerate(chunks):
+        each(max(low, 1), high, lambda step: passage(step).wait_recv())
+        block = lax.dot_general(
+            flat[low * PBLK:high * PBLK, :], q[...], (((1,), (1,)), ((), ())),
+            preferred_element_type=jnp.float32,
+        )
+        place, size = packed(index)
+        part[pl.ds(place.start, size), :] = block[:, :LANES]
+        part[pl.ds(place.start + size, size // 2), :] = jnp.concatenate(
+            [block[:size // 2, LANES:], block[size // 2:, LANES:]], axis=1
+        )
+        for step in reversed(range(1, m)):
+            score(index, step).start()
+
+    def swap(row):
+        return jnp.concatenate([row[:, LANES // 2:], row[:, :LANES // 2]], axis=1)
+
+    spots = pos_ref[...] ^ (me * PBLK)
+    spots_a = spots[:, :LANES]
+    spots_b = jnp.concatenate([spots[:, LANES:], spots[:, LANES:]], axis=1)
+    scores_a, scores_b, hits_a, hits_b = [], [], [], []
+    for index, (low, high) in enumerate(chunks):
+        place, size = packed(index)
+        for step in range(1, m):
+            score(index, step).wait_recv()
+        terms = [part[place, :]] + [shares[step, place, :] for step in range(1, m)]
+        while len(terms) > 1:
+            terms = [first + second for first, second in zip(terms[::2], terms[1::2])]
+        scores_a.append(terms[0][:size])
+        scores_b.append(terms[0][size:])
+        down = lax.broadcasted_iota(jnp.int32, (size, LANES), 0) + low * PBLK
+        hits_a.append(down == spots_a)
+        down = lax.broadcasted_iota(jnp.int32, (size // 2, LANES), 0) + low * PBLK
+        right = lax.broadcasted_iota(jnp.int32, (size // 2, LANES), 1) // (LANES // 2)
+        hits_b.append(down + right * (size // 2) == spots_b)
+
+    def gathered(blocks, combine, reduce):
+        return functools.reduce(combine, [reduce(block, axis=0, keepdims=True) for block in blocks])
+
+    def softmax(scores, hits, paired):
+        top = gathered(scores, jnp.maximum, jnp.max)
+        if paired:
+            top = jnp.maximum(top, swap(top))
+        raised = [jnp.exp(block - top) for block in scores]
+        total = gathered(raised, jnp.add, jnp.sum)
+        picked = [jnp.where(hit, block, 0.0) for hit, block in zip(hits, scores)]
+        positive = gathered(picked, jnp.add, jnp.sum)
+        if paired:
+            total = total + swap(total)
+            positive = positive + swap(positive)
+        inverse = 1.0 / total
+        weights = [
+            (block * inverse - hit.astype(jnp.float32)).astype(jnp.bfloat16)
+            for block, hit in zip(raised, hits)
+        ]
+        return weights, top + jnp.log(total) - positive
+
+    weights_a, losses_a = softmax(scores_a, hits_a, False)
+    weights_b, losses_b = softmax(scores_b, hits_b, True)
+    for (low, high), first, second in zip(chunks, weights_a, weights_b):
+        start, size = low * PBLK, (high - low) * PBLK
+        turned[pl.ds(start, size), pl.ds(0, LANES)] = first
+        rest = pl.ds(LANES, LANES // 2)
+        turned[pl.ds(start, size // 2), rest] = second[:, :LANES // 2]
+        turned[pl.ds(start + size // 2, size // 2), rest] = second[:, LANES // 2:]
 
     def slim(step):
         return remote(
@@ -199,9 +213,8 @@
     each(half // group, n // group, give_slim)
     each(0, half // group, give_wide)
 
-    for step in range(1, m):
-        loss_beside(step).wait_recv()
-    loss_dp[0] = jnp.sum(loss_mp[...], axis=0)
+    losses = losses_a + 0.5 * losses_b
+    loss_dp[0] = jnp.broadcast_to(jnp.sum(losses, axis=1, keepdims=True), loss_dp.shape[1:])
 
     def loss_across(step):
         return remote(
@@ -210,7 +223,9 @@
 
     each(1, n, lambda step: loss_across(step).start())
 
-    qgrad_ref[...] = jnp.dot(weights[...], flat[...], preferred_element_type=jnp.float32)
+    qgrad_ref[...] = lax.dot_general(
+        turned[...], flat[...], (((0,), (0,)), ((), ())), preferred_element_type=jnp.float32
+    )
     save_q = pltpu.make_async_copy(qgrad_ref, qgrad_hbm, local_sem.at[4])
     save_q.start()
 
@@ -235,7 +250,11 @@
     save_p = pltpu.make_async_copy(pgrad_ref, pgrad_hbm, local_sem.at[5])
     save_p.start()
     each(1, n, lambda step: loss_across(step).wait_recv())
-    loss_ref[...] = jnp.sum(loss_dp[...], axis=0)[0:1, 0:1] / (rows * n)
+    losses = loss_dp[...]
+    while losses.shape[0] > 1:
+        losses = losses.reshape(losses.shape[0] // 2, 2, *losses.shape[1:])
+        losses = losses[:, 0] + losses[:, 1]
+    loss_ref[...] = losses[0, 0:1, 0:1] / (rows * n)
     save_loss = pltpu.make_async_copy(loss_ref, loss_hbm, local_sem.at[6])
     save_loss.start()
 
@@ -246,10 +265,9 @@
     each(1, n, settle)
     each(1, half, lambda step: wide(step).wait_send())
     each(half, n, lambda step: slim(step).wait_send())
-    for step in range(1, m):
-        score(step).wait_send()
-        weight(step).wait_send()
-        loss_beside(step).wait_send()
+    for index in range(len(chunks)):
+        for step in range(1, m):
+            score(index, step).wait_send()
     save_q.wait()
     save_p.wait()
     save_loss.wait()
@@ -277,7 +295,7 @@
 
 def per_device(n, m, queries, passages, pair_block, positives):
     rows, width = queries.shape
-    half, share, cands = n // 2, rows // m, n * PBLK
+    half, cands = n // 2, n * PBLK
     vmem, sems = pltpu.VMEM, pltpu.SemaphoreType.DMA
     bf16, f32 = jnp.bfloat16, jnp.float32
     results = [
@@ -288,25 +306,22 @@
     held = [vmem((1, 1), f32), vmem((rows, width), f32), vmem(passages.shape, f32)]
     scratch = held + [
         pltpu.SMEM((n,), jnp.int32),
-        pltpu.SMEM((rows,), jnp.int32),
+        vmem((1, rows), jnp.int32),
         vmem((rows, width), bf16),
         vmem((PB_DEV, PBLK, width), bf16),
         vmem((n, PBLK, width), bf16),
         vmem((cands, width), bf16),
-        vmem((rows, cands), f32),
-        vmem((m, share, cands), f32),
-        vmem((rows, cands), bf16),
+        vmem((cands * 3 // 2, LANES), f32),
+        vmem((m, cands * 3 // 2, LANES), f32),
         vmem((cands, rows), bf16),
-        vmem((share, cands), f32),
         vmem((half, PBLK, width), f32),
         vmem((half, PBLK, width), bf16),
         vmem((half, PBLK, width), f32),
         vmem((half, PBLK, width), bf16),
-        vmem((m, 8, 128), f32),
         vmem((n, 8, 128), f32),
         sems((7,)),
-        sems((n,)), sems((n,)), sems((m,)), sems((m,)), sems((m,)), sems((m,)),
-        sems((m,)), sems((m,)), sems((n,)), sems((n,)), sems((n,)), sems((n,)),
+        sems((n,)), sems((n,)), sems((3, m)), sems((3, m)),
+        sems((n,)), sems((n,)), sems((n,)), sems((n,)),
     ]
     anywhere = pl.BlockSpec(memory_space=pl.ANY)
     found = pl.pallas_call(
@@ -319,7 +334,8 @@
             collective_id=0, has_side_effects=True,
             vmem_limit_bytes=60 << 20,
         ),
-    )(queries, passages.reshape(PB_DEV, PBLK, width), pair_block.reshape(n), positives)
+    )(queries, passages.reshape(PB_DEV, PBLK, width), pair_block.reshape(n),
+      positives.reshape(1, rows))
     loss, query_grad, passage_grad = pl.pallas_call(
         hand_over,
         out_shape=results,

time: 33.3 us -> 31.4 us (0.943)
  Pallas kernels: 32.5 us -> 30.6 us
    pallas_call x1, Pallas kernels: 29.9 us -> 28 us  [per_device(): pl.pallas_call(functools.partial(kernel, n, m), out_shape=results, in_spe...]
where the time goes in v4:
time: 31.4 us; the launch traced here: 31.3 us
  Pallas kernels  30.6 us (97%)
  between operations  0.64 us (2%)
    pallas_call x1, Pallas kernels, per_device(): pl.pallas_call(functools.partial(kernel, n, m), out_shape=results, in_spe...  28 us
    pallas_call x1, Pallas kernels, per_device(): pl.pallas_call(hand_over, out_shape=results, in_specs=[anywhere] * 3, out...  2.64 us

profile of v4, /device:TPU:0, one launch (start us, length us, event | category | flops | bytes accessed | tf_op | source)
XLA Modules:
  0.0 31.3 jit_solution(18159116130446513113)
XLA Ops:
  0.6 28.0 %shard_map.67 = (f32[1,1]{1,0:T(1,128)}, f32[192,1024]{1,0:T(8,128)}, f32[64,1024]{1,0:T(8,128)}) custom-call(bf16[192,1024]{1,0:T(8,128)(2,1)} %q_hbm.1, bf16[4,16,1024]{2,1,0:T(8,128)(2,1)} %bitcast.4, s32[8]{0:T(128)} %bitcast.6, s32[1,192]{1,0:T(1,128)} %bitcast.5), custom_call_target="tpu_custom_call" | custom-call | tf_op jit(solution)/shard_map/pallas_call | solution.py:327
  28.6 2.6 %shard_map.68 = (f32[1,1]{1,0:T(1,128)}, f32[192,1024]{1,0:T(8,128)}, f32[64,1024]{1,0:T(8,128)}) custom-call(f32[1,1]{1,0:T(1,128)} %get-tuple-element.9.loss_in, f32[192,1024]{1,0:T(8,128)} %get-tuple-element.10.qgrad_in, f32[64,1024]{1,0:T(8,128)} %get-tuple-element.11.pgrad_in), custom_call_target="tpu_custom_call" | custom-call | tf_op jit(solution)/shard_map/pallas_call | solution.py:339

commit v5 on v4

--- a/solution.py
+++ b/solution.py
@@ -91,8 +91,9 @@
             outgoing.at[step], flat.at[slot(step)], a_send.at[step], a_recv.at[step], across(step)
         )
 
-    each(half, n, lambda step: passage(step).start())
+    passage(half).start()
     each(1, half, lambda step: passage(step).start())
+    each(half + 1, n, lambda step: passage(step).start())
 
     load_pos.wait()
     load_q.wait()
@@ -229,6 +230,10 @@
     save_q = pltpu.make_async_copy(qgrad_ref, qgrad_hbm, local_sem.at[4])
     save_q.start()
 
+    each(1, n, lambda step: passage(step).wait_send())
+    for index in range(len(chunks)):
+        for step in range(1, m):
+            score(index, step).wait_send()
     pgrad_ref[...] = jnp.zeros_like(pgrad_ref)
 
     def collect(step, block):
@@ -258,16 +263,9 @@
     save_loss = pltpu.make_async_copy(loss_ref, loss_hbm, local_sem.at[6])
     save_loss.start()
 
-    def settle(step):
-        passage(step).wait_send()
-        loss_across(step).wait_send()
-
-    each(1, n, settle)
+    each(1, n, lambda step: loss_across(step).wait_send())
     each(1, half, lambda step: wide(step).wait_send())
     each(half, n, lambda step: slim(step).wait_send())
-    for index in range(len(chunks)):
-        for step in range(1, m):
-            score(index, step).wait_send()
     save_q.wait()
     save_p.wait()
     save_loss.wait()

time: 31.4 us -> 31.1 us (level)
  no operation moved by 1% of the time
where the time goes in v5:
time: 31.1 us; the launch traced here: 31 us
  Pallas kernels  30.3 us (97%)
  between operations  0.64 us (2%)
    pallas_call x1, Pallas kernels, per_device(): pl.pallas_call(functools.partial(kernel, n, m), out_shape=results, in_spe...  27.7 us
    pallas_call x1, Pallas kernels, per_device(): pl.pallas_call(hand_over, out_shape=results, in_specs=[anywhere] * 3, out...  2.64 us

profile of v5, /device:TPU:0, one launch (start us, length us, event | category | flops | bytes accessed | tf_op | source)
XLA Modules:
  0.0 31.0 jit_solution(3598659416238120938)
XLA Ops:
  0.6 27.7 %shard_map.67 = (f32[1,1]{1,0:T(1,128)}, f32[192,1024]{1,0:T(8,128)}, f32[64,1024]{1,0:T(8,128)}) custom-call(bf16[192,1024]{1,0:T(8,128)(2,1)} %q_hbm.1, bf16[4,16,1024]{2,1,0:T(8,128)(2,1)} %bitcast.4, s32[8]{0:T(128)} %bitcast.6, s32[1,192]{1,0:T(1,128)} %bitcast.5), custom_call_target="tpu_custom_call" | custom-call | tf_op jit(solution)/shard_map/pallas_call | solution.py:325
  28.3 2.6 %shard_map.68 = (f32[1,1]{1,0:T(1,128)}, f32[192,1024]{1,0:T(8,128)}, f32[64,1024]{1,0:T(8,128)}) custom-call(f32[1,1]{1,0:T(1,128)} %get-tuple-element.9.loss_in, f32[192,1024]{1,0:T(8,128)} %get-tuple-element.10.qgrad_in, f32[64,1024]{1,0:T(8,128)} %get-tuple-element.11.pgrad_in), custom_call_target="tpu_custom_call" | custom-call | tf_op jit(solution)/shard_map/pallas_call | solution.py:337

commit v6 on v5

--- a/solution.py
+++ b/solution.py
@@ -20,6 +20,10 @@
         result = result + bit * (mine + other - 2 * mine * other)
         bit *= 2
     return result
+
+
+def wide_slots(count):
+    return count // 2 - count // 8
 
 
 def each(low, high, body):
@@ -98,7 +102,8 @@
     load_pos.wait()
     load_q.wait()
 
-    chunks = ((0, half), (half, half + n // 4), (half + n // 4, n))
+    ends = (0, half, half + n // 4, n - n // 8, n)
+    chunks = tuple(zip(ends[:-1], ends[1:]))
 
     def packed(index):
         low, high = chunks[index]
@@ -178,41 +183,38 @@
         turned[pl.ds(start, size // 2), rest] = second[:, :LANES // 2]
         turned[pl.ds(start + size // 2, size // 2), rest] = second[:, LANES // 2:]
 
-    def slim(step):
-        return remote(
-            sent_slim.at[step - half], got_slim.at[step - half], e_send.at[step], e_recv.at[step],
-            across(step),
-        )
-
-    def wide(step):
-        return remote(
-            sent_wide.at[step], got_wide.at[step], e_send.at[step], e_recv.at[step], across(step)
-        )
+    wide = wide_slots(n)
+
+    def gradient(step, slim):
+        if slim:
+            source, target = sent_slim.at[step - wide], got_slim.at[step - wide]
+        else:
+            source, target = sent_wide.at[step], got_wide.at[step]
+        return remote(source, target, e_send.at[step], e_recv.at[step], across(step))
 
     group = min(half, 4)
 
-    def grads(index):
+    def give(index, slim):
         block = turned[pl.ds(index * group * PBLK, group * PBLK), :]
         result = jnp.dot(block, q[...], preferred_element_type=jnp.float32)
-        return result.reshape(group, PBLK, q.shape[1])
-
-    def give_slim(index):
-        sent_slim[pl.ds(index * group - half, group)] = grads(index).astype(jnp.bfloat16)
-        for place in range(group):
-            slim(index * group + place).start()
-
-    def give_wide(index):
-        sent_wide[pl.ds(index * group, group)] = grads(index)
+        result = result.reshape(group, PBLK, q.shape[1])
         for place in range(group):
             step = index * group + place
-            if isinstance(step, int):
-                if step:
-                    wide(step).start()
+            fixed = isinstance(step, int)
+            narrow = step >= wide if fixed else slim
+            if narrow:
+                sent_slim[step - wide] = result[place].astype(jnp.bfloat16)
             else:
-                pl.when(step > 0)(lambda step=step: wide(step).start())
-
-    each(half // group, n // group, give_slim)
-    each(0, half // group, give_wide)
+                sent_wide[step] = result[place]
+            if not fixed:
+                pl.when(step > 0)(lambda step=step: gradient(step, narrow).start())
+            elif step:
+                gradient(step, narrow).start()
+
+    wide_groups = -(-wide // group)
+    each(half // group, n // group, lambda index: give(index, True))
+    each(wide_groups, half // group, lambda index: give(index, True))
+    each(0, wide_groups, lambda index: give(index, False))
 
     losses = losses_a + 0.5 * losses_b
     loss_dp[0] = jnp.broadcast_to(jnp.sum(losses, axis=1, keepdims=True), loss_dp.shape[1:])
@@ -242,16 +244,16 @@
             pgrad_ref[pl.ds(place * PBLK, PBLK), :] += jnp.where(pick == place, block, 0.0)
 
     def take_wide(step):
-        wide(step).wait_recv()
+        gradient(step, False).wait_recv()
         collect(step, got_wide[step])
 
     def take_slim(step):
-        slim(step).wait_recv()
-        collect(step, got_slim[step - half].astype(jnp.float32))
+        gradient(step, True).wait_recv()
+        collect(step, got_slim[step - wide].astype(jnp.float32))
 
     collect(0, sent_wide[0])
-    each(1, half, take_wide)
-    each(half, n, take_slim)
+    each(1, wide, take_wide)
+    each(wide, n, take_slim)
     save_p = pltpu.make_async_copy(pgrad_ref, pgrad_hbm, local_sem.at[5])
     save_p.start()
     each(1, n, lambda step: loss_across(step).wait_recv())
@@ -264,20 +266,21 @@
     save_loss.start()
 
     each(1, n, lambda step: loss_across(step).wait_send())
-    each(1, half, lambda step: wide(step).wait_send())
-    each(half, n, lambda step: slim(step).wait_send())
+    each(1, wide, lambda step: gradient(step, False).wait_send())
+    each(wide, n, lambda step: gradient(step, True).wait_send())
     save_q.wait()
     save_p.wait()
     save_loss.wait()
 
 
 def hand_over(loss_in, qgrad_in, pgrad_in, loss_out, qgrad_out, pgrad_out, loss, qgrad, pgrad, sems):
-    parts = [(loss_in, loss, loss_out)]
-    piece = 64
+    parts = []
     for source, held, target in ((qgrad_in, qgrad, qgrad_out), (pgrad_in, pgrad, pgrad_out)):
+        piece = held.shape[0] // 2
         for start in range(0, held.shape[0], piece):
             place = pl.ds(start, piece)
             parts.append((source.at[place], held.at[place], target.at[place]))
+    parts.append((loss_in, loss, loss_out))
     loads, stores = [], []
     for index, (source, held, target) in enumerate(parts):
         loads.append(pltpu.make_async_copy(source, held, sems.at[0, index]))
@@ -293,7 +296,7 @@
 
 def per_device(n, m, queries, passages, pair_block, positives):
     rows, width = queries.shape
-    half, cands = n // 2, n * PBLK
+    wide, cands = wide_slots(n), n * PBLK
     vmem, sems = pltpu.VMEM, pltpu.SemaphoreType.DMA
     bf16, f32 = jnp.bfloat16, jnp.float32
     results = [
@@ -312,13 +315,13 @@
         vmem((cands * 3 // 2, LANES), f32),
         vmem((m, cands * 3 // 2, LANES), f32),
         vmem((cands, rows), bf16),
-        vmem((half, PBLK, width), f32),
-        vmem((half, PBLK, width), bf16),
-        vmem((half, PBLK, width), f32),
-        vmem((half, PBLK, width), bf16),
+        vmem((wide, PBLK, width), f32),
+        vmem((n - wide, PBLK, width), bf16),
+        vmem((wide, PBLK, width), f32),
+        vmem((n - wide, PBLK, width), bf16),
         vmem((n, 8, 128), f32),
         sems((7,)),
-        sems((n,)), sems((n,)), sems((3, m)), sems((3, m)),
+        sems((n,)), sems((n,)), sems((4, m)), sems((4, m)),
         sems((n,)), sems((n,)), sems((n,)), sems((n,)),
     ]
     anywhere = pl.BlockSpec(memory_space=pl.ANY)
@@ -339,7 +342,7 @@
         out_shape=results,
         in_specs=[anywhere] * 3,
         out_specs=[anywhere] * 3,
-        scratch_shapes=held + [sems((2, 1 + (rows + passages.shape[0]) // 64))],
+        scratch_shapes=held + [sems((2, 5))],
         compiler_params=pltpu.CompilerParams(vmem_limit_bytes=60 << 20),
     )(*found)
     return loss.reshape(()), query_grad, passage_grad

time: 31.1 us -> 30.6 us (0.984)
  Pallas kernels: 30.3 us -> 29.8 us
    pallas_call x1, Pallas kernels: 27.7 us -> 27.2 us  [per_device(): pl.pallas_call(functools.partial(kernel, n, m), out_shape=results, in_spe...]
where the time goes in v6:
time: 30.6 us; the launch traced here: 30.5 us
  Pallas kernels  29.8 us (97%)
  between operations  0.64 us (2%)
    pallas_call x1, Pallas kernels, per_device(): pl.pallas_call(functools.partial(kernel, n, m), out_shape=results, in_spe...  27.2 us
    pallas_call x1, Pallas kernels, per_device(): pl.pallas_call(hand_over, out_shape=results, in_specs=[anywhere] * 3, out...  2.67 us

profile of v6, /device:TPU:0, one launch (start us, length us, event | category | flops | bytes accessed | tf_op | source)
XLA Modules:
  0.0 30.5 jit_solution(1801679978958184312)
XLA Ops:
  0.6 27.2 %shard_map.67 = (f32[1,1]{1,0:T(1,128)}, f32[192,1024]{1,0:T(8,128)}, f32[64,1024]{1,0:T(8,128)}) custom-call(bf16[192,1024]{1,0:T(8,128)(2,1)} %q_hbm.1, bf16[4,16,1024]{2,1,0:T(8,128)(2,1)} %bitcast.4, s32[8]{0:T(128)} %bitcast.6, s32[1,192]{1,0:T(1,128)} %bitcast.5), custom_call_target="tpu_custom_call" | custom-call | tf_op jit(solution)/shard_map/pallas_call | solution.py:328
  27.8 2.7 %shard_map.68 = (f32[1,1]{1,0:T(1,128)}, f32[192,1024]{1,0:T(8,128)}, f32[64,1024]{1,0:T(8,128)}) custom-call(f32[1,1]{1,0:T(1,128)} %get-tuple-element.9.loss_in, f32[192,1024]{1,0:T(8,128)} %get-tuple-element.10.qgrad_in, f32[64,1024]{1,0:T(8,128)} %get-tuple-element.11.pgrad_in), custom_call_target="tpu_custom_call" | custom-call | tf_op jit(solution)/shard_map/pallas_call | solution.py:340

commit v7 on v6

--- a/solution.py
+++ b/solution.py
@@ -35,8 +35,7 @@
 
 
 def kernel(
-    n, m, q_hbm, p_hbm, pair_hbm, pos_hbm, loss_hbm, qgrad_hbm, pgrad_hbm,
-    loss_ref, qgrad_ref, pgrad_ref, pair_ref, pos_ref, q, p, outgoing, flat, part, shares, turned,
+    n, m, q_hbm, p_hbm, pair_hbm, pos_hbm, loss_ref, qgrad_ref, pgrad_ref, pair_ref, pos_ref, q, p, outgoing, flat, part, shares, turned,
     sent_wide, sent_slim, got_wide, got_slim, loss_dp,
     local_sem, a_send, a_recv, b_send, b_recv, e_send, e_recv, f_send, f_recv,
 ):
@@ -229,8 +228,6 @@
     qgrad_ref[...] = lax.dot_general(
         turned[...], flat[...], (((0,), (0,)), ((), ())), preferred_element_type=jnp.float32
     )
-    save_q = pltpu.make_async_copy(qgrad_ref, qgrad_hbm, local_sem.at[4])
-    save_q.start()
 
     each(1, n, lambda step: passage(step).wait_send())
     for index in range(len(chunks)):
@@ -254,44 +251,29 @@
     collect(0, sent_wide[0])
     each(1, wide, take_wide)
     each(wide, n, take_slim)
-    save_p = pltpu.make_async_copy(pgrad_ref, pgrad_hbm, local_sem.at[5])
-    save_p.start()
     each(1, n, lambda step: loss_across(step).wait_recv())
     losses = loss_dp[...]
     while losses.shape[0] > 1:
         losses = losses.reshape(losses.shape[0] // 2, 2, *losses.shape[1:])
         losses = losses[:, 0] + losses[:, 1]
-    loss_ref[...] = losses[0, 0:1, 0:1] / (rows * n)
-    save_loss = pltpu.make_async_copy(loss_ref, loss_hbm, local_sem.at[6])
-    save_loss.start()
+    loss_ref[...] = losses[0] / (rows * n)
 
     each(1, n, lambda step: loss_across(step).wait_send())
     each(1, wide, lambda step: gradient(step, False).wait_send())
     each(wide, n, lambda step: gradient(step, True).wait_send())
-    save_q.wait()
-    save_p.wait()
-    save_loss.wait()
-
-
-def hand_over(loss_in, qgrad_in, pgrad_in, loss_out, qgrad_out, pgrad_out, loss, qgrad, pgrad, sems):
-    parts = []
-    for source, held, target in ((qgrad_in, qgrad, qgrad_out), (pgrad_in, pgrad, pgrad_out)):
-        piece = held.shape[0] // 2
-        for start in range(0, held.shape[0], piece):
-            place = pl.ds(start, piece)
-            parts.append((source.at[place], held.at[place], target.at[place]))
-    parts.append((loss_in, loss, loss_out))
-    loads, stores = [], []
-    for index, (source, held, target) in enumerate(parts):
-        loads.append(pltpu.make_async_copy(source, held, sems.at[0, index]))
-        stores.append(pltpu.make_async_copy(held, target, sems.at[1, index]))
-    for load in loads:
-        load.start()
-    for load, store in zip(loads, stores):
-        load.wait()
-        store.start()
-    for store in stores:
-        store.wait()
+
+
+def hand_over(loss_in, qgrad_in, pgrad_in, loss_out, qgrad_out, pgrad_out, loss, sems):
+    loss[...] = loss_in[0:1, 0:1]
+    pairs = ((qgrad_in, qgrad_out), (pgrad_in, pgrad_out), (loss, loss_out))
+    copies = [
+        pltpu.make_async_copy(source, target, sems.at[index])
+        for index, (source, target) in enumerate(pairs)
+    ]
+    for copy in copies:
+        copy.start()
+    for copy in copies:
+        copy.wait()
 
 
 def per_device(n, m, queries, passages, pair_block, positives):
@@ -304,8 +286,8 @@
         jax.ShapeDtypeStruct((rows, width), f32),
         jax.ShapeDtypeStruct(passages.shape, f32),
     ]
-    held = [vmem((1, 1), f32), vmem((rows, width), f32), vmem(passages.shape, f32)]
-    scratch = held + [
+    held = [vmem((8, 128), f32), vmem((rows, width), f32), vmem(passages.shape, f32)]
+    scratch = [
         pltpu.SMEM((n,), jnp.int32),
         vmem((1, rows), jnp.int32),
         vmem((rows, width), bf16),
@@ -320,16 +302,17 @@
         vmem((wide, PBLK, width), f32),
         vmem((n - wide, PBLK, width), bf16),
         vmem((n, 8, 128), f32),
-        sems((7,)),
+        sems((4,)),
         sems((n,)), sems((n,)), sems((4, m)), sems((4, m)),
         sems((n,)), sems((n,)), sems((n,)), sems((n,)),
     ]
     anywhere = pl.BlockSpec(memory_space=pl.ANY)
+    inside = pl.BlockSpec(memory_space=pltpu.VMEM)
     found = pl.pallas_call(
         functools.partial(kernel, n, m),
-        out_shape=results,
+        out_shape=held,
         in_specs=[anywhere] * 4,
-        out_specs=[anywhere] * 3,
+        out_specs=[inside] * 3,
         scratch_shapes=scratch,
         compiler_params=pltpu.CompilerParams(
             collective_id=0, has_side_effects=True,
@@ -340,10 +323,10 @@
     loss, query_grad, passage_grad = pl.pallas_call(
         hand_over,
         out_shape=results,
-        in_specs=[anywhere] * 3,
+        in_specs=[inside, anywhere, anywhere],
         out_specs=[anywhere] * 3,
-        scratch_shapes=held + [sems((2, 5))],
-        compiler_params=pltpu.CompilerParams(vmem_limit_bytes=60 << 20),
+        scratch_shapes=[vmem((1, 1), f32), sems((3,))],
+        compiler_params=pltpu.CompilerParams(vmem_limit_bytes=1 << 20),
     )(*found)
     return loss.reshape(()), query_grad, passage_grad
 

time: 30.6 us -> 28.4 us (0.928)
  Pallas kernels: 29.8 us -> 27.6 us
    pallas_call x2, Pallas kernels: 29.8 us -> 27.6 us  [the longest x1 26.6 us: per_device(): pl.pallas_call(functools.partial(kernel, n, m), out_shape=held, in_specs=...]
where the time goes in v7:
time: 28.4 us; the launch traced here: 28.3 us
  Pallas kernels  27.6 us (97%)
  between operations  0.64 us (2%)
    pallas_call x1, Pallas kernels, per_device(): pl.pallas_call(functools.partial(kernel, n, m), out_shape=held, in_specs=...  26.6 us
    pallas_call x1, Pallas kernels, per_device(): pl.pallas_call(hand_over, out_shape=results, in_specs=[inside, anywhere,...  0.99 us

profile of v7, /device:TPU:0, one launch (start us, length us, event | category | flops | bytes accessed | tf_op | source)
XLA Modules:
  0.0 28.3 jit_solution(10363427596301064653)
XLA Ops:
  0.6 26.6 %shard_map.67 = (f32[8,128]{1,0:T(8,128)S(1)}, f32[192,1024]{1,0:T(8,128)S(1)}, f32[64,1024]{1,0:T(8,128)S(1)}) custom-call(bf16[192,1024]{1,0:T(8,128)(2,1)} %q_hbm.1, bf16[4,16,1024]{2,1,0:T(8,128)(2,1)} %bitcast.4, s32[8]{0:T(128)} %bitcast.6, s32[1,192]{1,0:T(1,128)} %bitcast.5), custom_call_target="tpu_custom_call" | custom-call | tf_op jit(solution)/shard_map/pallas_call | solution.py:311
  27.3 1.0 %shard_map.68 = (f32[1,1]{1,0:T(1,128)}, f32[192,1024]{1,0:T(8,128)}, f32[64,1024]{1,0:T(8,128)}) custom-call(f32[8,128]{1,0:T(8,128)S(1)} %get-tuple-element.9.loss_in, f32[192,1024]{1,0:T(8,128)S(1)} %get-tuple-element.10.qgrad_in, f32[64,1024]{1,0:T(8,128)S(1)} %get-tuple-element.11.pgrad_in), custom_call_target="tpu_custom_call" | custom-call | tf_op jit(solution)/shard_map/pallas_call | solution.py:323

commit v8 on v7

--- a/solution.py
+++ b/solution.py
@@ -207,13 +207,25 @@
                 sent_wide[step] = result[place]
             if not fixed:
                 pl.when(step > 0)(lambda step=step: gradient(step, narrow).start())
-            elif step:
-                gradient(step, narrow).start()
+
+    def begin(*steps):
+        for step in steps:
+            gradient(step, step >= wide).start()
 
     wide_groups = -(-wide // group)
-    each(half // group, n // group, lambda index: give(index, True))
-    each(wide_groups, half // group, lambda index: give(index, True))
-    each(0, wide_groups, lambda index: give(index, False))
+    if n <= UNROLL:
+        order = [step for near in range(half) for step in (near, half + near)][1:]
+        early = [half, half + 1]
+        for index in range(half // group, n // group):
+            give(index, True)
+        begin(*early)
+        for index in range(half // group):
+            give(index, False)
+        begin(*[step for step in order if step not in early])
+    else:
+        lax.fori_loop(half // group, n // group, lambda index, carry: (give(index, True), carry)[1], 0)
+        lax.fori_loop(wide_groups, half // group, lambda index, carry: (give(index, True), carry)[1], 0)
+        lax.fori_loop(0, wide_groups, lambda index, carry: (give(index, False), carry)[1], 0)
 
     losses = losses_a + 0.5 * losses_b
     loss_dp[0] = jnp.broadcast_to(jnp.sum(losses, axis=1, keepdims=True), loss_dp.shape[1:])

time: 28.4 us -> 28.4 us (level)
  no operation moved by 1% of the time
where the time goes in v8:
time: 28.4 us; the launch traced here: 28.3 us
  Pallas kernels  27.6 us (97%)
  between operations  0.64 us (2%)
    pallas_call x1, Pallas kernels, per_device(): pl.pallas_call(functools.partial(kernel, n, m), out_shape=held, in_specs=...  26.6 us
    pallas_call x1, Pallas kernels, per_device(): pl.pallas_call(hand_over, out_shape=results, in_specs=[inside, anywhere,...  0.99 us

profile of v8, /device:TPU:0, one launch (start us, length us, event | category | flops | bytes accessed | tf_op | source)
XLA Modules:
  0.0 28.3 jit_solution(10534813344943140745)
XLA Ops:
  0.6 26.6 %shard_map.67 = (f32[8,128]{1,0:T(8,128)S(1)}, f32[192,1024]{1,0:T(8,128)S(1)}, f32[64,1024]{1,0:T(8,128)S(1)}) custom-call(bf16[192,1024]{1,0:T(8,128)(2,1)} %q_hbm.1, bf16[4,16,1024]{2,1,0:T(8,128)(2,1)} %bitcast.4, s32[8]{0:T(128)} %bitcast.6, s32[1,192]{1,0:T(1,128)} %bitcast.5), custom_call_target="tpu_custom_call" | custom-call | tf_op jit(solution)/shard_map/pallas_call | solution.py:323
  27.3 1.0 %shard_map.68 = (f32[1,1]{1,0:T(1,128)}, f32[192,1024]{1,0:T(8,128)}, f32[64,1024]{1,0:T(8,128)}) custom-call(f32[8,128]{1,0:T(8,128)S(1)} %get-tuple-element.9.loss_in, f32[192,1024]{1,0:T(8,128)S(1)} %get-tuple-element.10.qgrad_in, f32[64,1024]{1,0:T(8,128)S(1)} %get-tuple-element.11.pgrad_in), custom_call_target="tpu_custom_call" | custom-call | tf_op jit(solution)/shard_map/pallas_call | solution.py:335

commit v9 on v7

--- a/solution.py
+++ b/solution.py
@@ -94,9 +94,7 @@
             outgoing.at[step], flat.at[slot(step)], a_send.at[step], a_recv.at[step], across(step)
         )
 
-    passage(half).start()
-    each(1, half, lambda step: passage(step).start())
-    each(half + 1, n, lambda step: passage(step).start())
+    each(1, n, lambda step: passage(step).start())
 
     load_pos.wait()
     load_q.wait()

time: 28.4 us -> 28.4 us (level)
  no operation moved by 1% of the time
where the time goes in v9:
time: 28.4 us; the launch traced here: 28.3 us
  Pallas kernels  27.6 us (97%)
  between operations  0.64 us (2%)
    pallas_call x1, Pallas kernels, per_device(): pl.pallas_call(functools.partial(kernel, n, m), out_shape=held, in_specs=...  26.6 us
    pallas_call x1, Pallas kernels, per_device(): pl.pallas_call(hand_over, out_shape=results, in_specs=[inside, anywhere,...  0.99 us

profile of v9, /device:TPU:0, one launch (start us, length us, event | category | flops | bytes accessed | tf_op | source)
XLA Modules:
  0.0 28.3 jit_solution(15308791877197001124)
XLA Ops:
  0.6 26.6 %shard_map.67 = (f32[8,128]{1,0:T(8,128)S(1)}, f32[192,1024]{1,0:T(8,128)S(1)}, f32[64,1024]{1,0:T(8,128)S(1)}) custom-call(bf16[192,1024]{1,0:T(8,128)(2,1)} %q_hbm.1, bf16[4,16,1024]{2,1,0:T(8,128)(2,1)} %bitcast.4, s32[8]{0:T(128)} %bitcast.6, s32[1,192]{1,0:T(1,128)} %bitcast.5), custom_call_target="tpu_custom_call" | custom-call | tf_op jit(solution)/shard_map/pallas_call | solution.py:309
  27.3 1.0 %shard_map.68 = (f32[1,1]{1,0:T(1,128)}, f32[192,1024]{1,0:T(8,128)}, f32[64,1024]{1,0:T(8,128)}) custom-call(f32[8,128]{1,0:T(8,128)S(1)} %get-tuple-element.9.loss_in, f32[192,1024]{1,0:T(8,128)S(1)} %get-tuple-element.10.qgrad_in, f32[64,1024]{1,0:T(8,128)S(1)} %get-tuple-element.11.pgrad_in), custom_call_target="tpu_custom_call" | custom-call | tf_op jit(solution)/shard_map/pallas_call | solution.py:321
